TPU v7x, 32 devices: a whole 2x2x4 slice. The times are simulated.
32 devices in a mesh: groups: 2 (over x), head: 16 (over z, y, core).
Axes of the slice: x: 2, y: 2, z: 4, core: 2. Of those that a mesh axis runs over, the one named last changes fastest.
Arguments:
- queries: bfloat16 [256, 2048], P('groups', 'head'), parts along dimension 0, may hold values from -400 to 400
- cache: bfloat16 [2, 8192, 128], P(None, ('groups', 'head')), parts along dimension 1, may hold values from -5 to 5
- cache_scale: bfloat16 [2, 1, 8192], P(None, None, ('groups', 'head')), parts along dimension 2, may hold values from 0.5 to 4
- offsets: int32 [4], P('groups'), parts along dimension 0, may hold values from 0 to 2048, as said below
- lengths: int32 [4], P('groups'), parts along dimension 0, may hold values from 64 to 2048, as said below
- clamp_code: int32 [2], P('groups'), parts along dimension 0, may hold values from 512 to 1535
- w_out: bfloat16 [2048, 16384], P('head'), may hold values from -0.125 to 0.125
Outputs:
- projected: bfloat16 [16384, 256], P('head', 'groups'), parts along dimension 1
There are 2 independent parts, one for each index of `groups`. A program takes and returns all parts, laid end to end along the dimension named above; an argument that names none is the same for every part. Nothing has to cross between parts.
Inputs may be any that keep to these rules, and one draw needn't show every extreme that they name: Request r's cache region is offsets[r] to offsets[r] + lengths[r] - 1 and lies within positions r * 2048 to (r + 1) * 2048 - 1. `lengths`: the last 64 positions of each region hold the span's own keys and values; in every draw some request's length is exactly 2048.
All inputs are finite; a program needn't handle non-finite values.
Results may differ from a plain program's by a relative error of at most 0.0068.
Values may be sent and summed in bfloat16 or wider, within the bound.
A program may use at most 128 MiB of HBM per device.

v0:
```python
import math

import jax
import jax.numpy as jnp
from jax import lax
from jax.sharding import PartitionSpec as P

SPAN = 64


NEG_FILL = -1e30


def hadamard(matrix_size):
    counter_index = jnp.arange(matrix_size, dtype=jnp.int32)
    common = counter_index[:, None] & counter_index[None, :]
    parity = jnp.zeros((matrix_size, matrix_size), jnp.int32)
    for bit_place in range(matrix_size.bit_length() - 1):
        parity = parity + (common >> bit_place & 1)
    return jnp.where(parity % 2 == 0, 1.0, -1.0).astype(jnp.float32)


def masked_scores(query_block, key_rows, key_scale, visible_tile, inv_root):
    scores = jnp.einsum("tjd,pd->jtp", query_block, key_rows, preferred_element_type=jnp.float32)
    scores = scores * (key_scale.astype(jnp.float32) * inv_root)[None, None, :]
    return jnp.where(visible_tile[None], scores, NEG_FILL)


def tile_sums(masked, row_max, visible_tile, value_scale, value_rows):
    weights = jnp.where(visible_tile[None], jnp.exp(masked - row_max[..., None]), 0.0)
    prob_rows = (weights * value_scale.astype(jnp.float32)[None, None, :]).astype(jnp.bfloat16)
    numerator = jnp.einsum("jtp,pd->jtd", prob_rows, value_rows, preferred_element_type=jnp.float32)
    return (numerator, jnp.sum(weights, axis=2))


def per_device(queries, cache, cache_scale, offsets, lengths, clamp_code, w_out):
    my_index = lax.axis_index("head")
    head_dim = queries.shape[1]
    local_len = cache.shape[1]
    kv_count = cache.shape[2] // head_dim
    gathered = lax.all_gather(queries, "head", axis=1, tiled=True)
    tok_rows = gathered.shape[0]
    head_count = gathered.shape[1] // head_dim
    per_group = head_count // kv_count
    token_ids = jnp.arange(tok_rows, dtype=jnp.int32)
    request = token_ids // SPAN
    within = token_ids % SPAN
    req_match = request[:, None] == jnp.arange(offsets.shape[0], dtype=jnp.int32)[None, :]
    starts = jnp.sum(jnp.where(req_match, offsets[None, :], 0), axis=1)
    last_pos = starts + jnp.sum(jnp.where(req_match, lengths[None, :], 0), axis=1) - SPAN + within
    inv_root = 1.0 / math.sqrt(head_dim)
    positions = my_index * local_len + jnp.arange(local_len, dtype=jnp.int32)
    visible = (positions[None, :] >= starts[:, None]) & (positions[None, :] <= last_pos[:, None])
    max_parts = []
    for kv_index in range(kv_count):
        column_left = kv_index * head_dim
        query_block = gathered[
            :, column_left * per_group : (column_left + head_dim) * per_group
        ].reshape(tok_rows, per_group, head_dim)
        masked = masked_scores(
            query_block,
            cache[0, :, column_left : column_left + head_dim],
            cache_scale[0, kv_index],
            visible,
            inv_root,
        )
        max_parts.append(jnp.max(masked, axis=2))
    local_max = jnp.concatenate(max_parts, 0)
    global_max = lax.pmax(local_max, "head")
    numer_parts = []
    denom_parts = []
    for kv_index in range(kv_count):
        column_left = kv_index * head_dim
        query_block = gathered[
            :, column_left * per_group : (column_left + head_dim) * per_group
        ].reshape(tok_rows, per_group, head_dim)
        masked = masked_scores(
            query_block,
            cache[0, :, column_left : column_left + head_dim],
            cache_scale[0, kv_index],
            visible,
            inv_root,
        )
        row_max = global_max[kv_index * per_group : (kv_index + 1) * per_group]
        numer_part, denom_part = tile_sums(
            masked,
            row_max,
            visible,
            cache_scale[1, kv_index],
            cache[1, :, column_left : column_left + head_dim],
        )
        numer_parts.append(numer_part)
        denom_parts.append(denom_part)
    numerator = jnp.concatenate(numer_parts, 0)
    denominator = jnp.concatenate(denom_parts, 0)
    numer_rows, denom_rows = (
        lax.psum_scatter(numerator, "head", scatter_dimension=1, tiled=True),
        lax.psum_scatter(denominator, "head", scatter_dimension=1, tiled=True),
    )
    token_attention = (numer_rows / denom_rows[..., None]).astype(jnp.bfloat16)
    clip_limit = clamp_code[0].astype(jnp.float32) / 1024.0
    scale_out = 1.0 / math.sqrt(head_count * head_dim)
    hd_matrix = hadamard(head_dim).astype(jnp.bfloat16)
    inner_mixed = jnp.einsum(
        "hrd,de->hre", token_attention, hd_matrix, preferred_element_type=jnp.float32
    )
    rotated = jnp.einsum(
        "gh,hre->gre", hadamard(head_count), inner_mixed, precision=lax.Precision.HIGHEST
    )
    clamped = jnp.clip(rotated * scale_out, -clip_limit, clip_limit).astype(jnp.bfloat16)
    activation = lax.all_to_all(clamped, "head", split_axis=0, concat_axis=1, tiled=True)[0]
    projected = lax.psum_scatter(
        lax.dot_general(
            w_out, activation, (((0,), (1,)), ((), ())), preferred_element_type=jnp.float32
        ),
        "head",
        scatter_dimension=0,
        tiled=True,
    )
    return projected.astype(jnp.bfloat16)


def solution(mesh):
    return jax.shard_map(
        per_device,
        mesh=mesh,
        in_specs=(
            P("groups", "head"),
            P(None, ("groups", "head"), None),
            P(None, None, ("groups", "head")),
            P("groups"),
            P("groups"),
            P("groups"),
            P("head", None),
        ),
        out_specs=P("head", "groups"),
        check_vma=False,
    )
```

profile of v0, /device:TPU:0, one launch (start us, length us, event | category | flops | bytes accessed | tf_op | source)
XLA Modules:
  0.0 252.1 jit_solution(6421445603097386101)
XLA Ops:
  6.5 0.0 copy-start
  6.5 0.0 reduce-scatter.4.cloned.1.call-start
  6.5 0.7 slice_convert_fusion
  7.3 0.7 convert_multiply_fusion
  7.9 0.9 copy.19
  8.8 24.6 %all_gather.3 = bf16[128,2048]{0,1:T(8,128)(2,1)S(1)} all-gather(bf16[128,128]{0,1:T(8,128)(2,1)S(1)} %copy.19), channel_id=1, replica_groups=mesh['groups'=2,'head'=16] {'head'}, dimensions={1}, use_global_device_ids=true | all-gather | bytes 557056 | tf_op jit(solution)/shard_map/all_gather | solution.py:41
  33.4 0.8 select_reduce_fusion
  34.2 0.1 compare_and_fusion
  34.3 1.3 fusion
  35.6 30.3 %pmax.7 = f32[16,128]{1,0:T(8,128)S(1)} all-reduce(f32[16,128]{1,0:T(8,128)S(1)} %get-tuple-element.7), channel_id=1, replica_groups=mesh['groups'=2,'head'=16] {'head'}, use_global_device_ids=true, to_apply=%region_3.4 | all-reduce | flops 2048 | bytes 16384 | tf_op jit(solution)/shard_map/pmax | solution.py:69
  65.9 0.0 copy-done
  65.9 0.0 copy-start.1
  65.9 1.9 fusion.5
  67.9 0.0 reduce-scatter.4.cloned.1.call-update
  67.9 0.0 reduce-scatter.6.cloned.1.call-start
  68.6 0.0 copy-done.1
  68.6 0.6 dynamic-slice
  69.8 0.6 fusion.1
  70.4 30.1 %all-reduce = f32[16,128]{1,0:T(8,128)S(1)} all-reduce(f32[16,128]{1,0:T(8,128)S(1)} %fusion.1), channel_id=3, replica_groups=mesh['groups'=2,'head'=16] {'head'}, use_global_device_ids=true, to_apply=%region_6.7.clone | all-reduce | flops 2048 | bytes 16384
  100.5 0.1 constant_dynamic-slice_fusion
  100.6 22.2 %reduce-scatter.4.cloned.1.call-done = f32[16,8,128]{2,1,0:T(8,128)} async-done(((f32[16,128,128]{2,1,0:T(8,128)}), f32[16,8,128]{2,1,0:T(8,128)}) %reduce-scatter.4.cloned.1.call-update) | async-done | bytes 65552 | tf_op jit(solution)/shard_map/reduce_scatter | solution.py:97
  122.8 0.9 divide_convert_fusion
  123.8 0.2 fusion.14
  124.0 0.2 fusion.4
  124.2 10.2 %all_to_all.4 = bf16[16,8,128]{2,1,0:T(8,128)(2,1)S(1)} all-to-all(bf16[16,8,128]{2,1,0:T(8,128)(2,1)S(1)} %copy.23), channel_id=1, replica_groups=mesh['groups'=2,'head'=16] {'head'}, dimensions={0} | all-to-all | bytes 65536 | tf_op jit(solution)/shard_map/all_to_all | solution.py:111
  134.4 6.7 %convolution_bitcast_fusion = f32[16384,128]{0,1:T(8,128)} fusion(bf16[128,16384]{1,0:T(8,128)(2,1)} %param.13, bf16[16,8,128]{2,1,0:T(8,128)(2,1)S(1)} %all_to_all.4), kind=kOutput, calls=%fused_computation | convolution fusion | flops 536870912 | bytes 12615680 | tf_op jit(solution)/shard_map/dot_general | solution.py:113
  141.1 0.0 reduce-scatter.6.cloned.1.call-update
  141.1 102.2 %reduce-scatter.6.cloned.1.call-done = f32[1024,128]{0,1:T(8,128)} async-done(((f32[16384,128]{0,1:T(8,128)}), f32[1024,128]{0,1:T(8,128)}) %reduce-scatter.6.cloned.1.call-update) | async-done | bytes 524304 | tf_op jit(solution)/shard_map/reduce_scatter | solution.py:112
  243.3 1.1 convert_element_type.32
  244.4 0.8 copy.24
  (4 shorter events, 0.0 us)
Async XLA Ops:
  6.5 59.4 %copy-start = (bf16[2,256,128]{2,1,0:T(8,128)(2,1)S(1)}, bf16[2,256,128]{2,1,0:T(8,128)(2,1)}, u32[]{:S(2)}) copy-start(bf16[2,256,128]{2,1,0:T(8,128)(2,1)} %param.8) | copy-start | bytes 393220
  6.5 116.3 %reduce-scatter.4.cloned.1.call-start = ((), (), s32[]{:S(2)}) async-start(), calls=%async_computation.3 | async-start | bytes 1114112 | tf_op jit(solution)/shard_map/reduce_scatter | solution.py:97
  65.9 2.7 %copy-start.1 = (u32[32]{0:T(128)S(1)}, u32[32]{0:T(128)}, u32[]{:S(2)}) copy-start(u32[32]{0:T(128)} %constant.97) | copy-start | bytes 388
  67.9 175.4 %reduce-scatter.6.cloned.1.call-start = ((), (), s32[]{:S(2)}) async-start(), calls=%async_computation.4 | async-start | bytes 8912896 | tf_op jit(solution)/shard_map/reduce_scatter | solution.py:112
Sparse Core Ops, SparseCore 0:
  68.0 54.7 reduce-scatter.3
  141.2 102.0 reduce-scatter.5
where the time goes:
time: 253 us; the launch traced here: 252 us
  waiting for transfers between devices  124 us (49%)
  blocking collectives  95.3 us (38%)
  between operations  14.8 us (6%)
  matrix products  10.3 us (4%)
  other arithmetic  4.83 us (2%)
    reduce_scatter x1, waiting for transfers between devices, per_device(): lax.psum_scatter(lax.dot_general(w_out, activation, (((0,), (1,)), ((), (...  102 us
    pmax x1, blocking collectives, per_device(): global_max = lax.pmax(local_max, 'head')  30.3 us
    unnamed x1, blocking collectives  30.1 us
    all_gather x1, blocking collectives, per_device(): gathered = lax.all_gather(queries, 'head', axis=1, tiled=True)  24.6 us
    reduce_scatter x1, waiting for transfers between devices, per_device(): lax.psum_scatter(numerator, 'head', scatter_dimension=1, tiled=True)  22.2 us
    all_to_all x1, blocking collectives, per_device(): lax.all_to_all(clamped, 'head', split_axis=0, concat_axis=1, tiled=True)[0]  10.2 us
    dot_general x1, matrix products, per_device(): lax.dot_general(w_out, activation, (((0,), (1,)), ((), ())), preferred_el...  6.66 us
  transfers between devices with their start and end apart: 2, of which 2 were waited for; matrix products, arithmetic and copies ran while one was open for 0% of the time, Pallas kernels for 0%

commit v1 on v0

--- a/solution.py
+++ b/solution.py
@@ -1,8 +1,11 @@
+import functools
 import math
 
 import jax
 import jax.numpy as jnp
 from jax import lax
+from jax.experimental import pallas as pl
+from jax.experimental.pallas import tpu as pltpu
 from jax.sharding import PartitionSpec as P
 
 SPAN = 64
@@ -33,7 +36,303 @@
     return (numerator, jnp.sum(weights, axis=2))
 
 
-def per_device(queries, cache, cache_scale, offsets, lengths, clamp_code, w_out):
+def fused_kernel(
+    n,
+    queries,
+    kv_own,
+    offsets,
+    lengths,
+    clamp_code,
+    w_out,
+    out,
+    kv_all,
+    scores,
+    att_all,
+    mix_send,
+    mix_recv,
+    core_send,
+    core_recv,
+    y_send,
+    y_recv,
+    z_send,
+    z_recv,
+    kv_zsem,
+    kv_ysem,
+    kv_csem,
+    kv_rsem,
+    att_ssem,
+    att_rsem,
+    mix_ssem,
+    mix_rsem,
+    core_ssem,
+    core_rsem,
+    y_ssem,
+    y_rsem,
+    z_ssem,
+    z_rsem,
+):
+    f32, bf16 = jnp.float32, jnp.bfloat16
+    rows = n // 4
+    tok_rows, head_dim = queries.shape
+    local_len = (kv_own.shape[0] - 16) // 2
+    scale_rows = local_len // head_dim
+    cols = out.shape[0]
+    me = lax.axis_index("head")
+    z, y, c = lax.div(me, 4), lax.rem(lax.div(me, 2), 2), lax.rem(me, 2)
+
+    def place(zz, yy, cc):
+        return zz * 4 + yy * 2 + cc
+
+    def z_at(step):
+        return lax.rem(z + step, rows)
+
+    y_peer, c_peer = place(z, 1 - y, c), place(z, y, 1 - c)
+    peers = [place(z_at(d), y, c) for d in range(1, rows)] + [y_peer, c_peer]
+
+    def remote(src, dst, ssem, rsem, peer):
+        return pltpu.make_async_remote_copy(
+            src_ref=src,
+            dst_ref=dst,
+            send_sem=ssem,
+            recv_sem=rsem,
+            device_id={"head": peer},
+            device_id_type=pl.DeviceIdType.MESH,
+        )
+
+    barrier = pltpu.get_barrier_semaphore()
+    for peer in peers:
+        pl.semaphore_signal(
+            barrier, inc=1, device_id={"head": peer}, device_id_type=pl.DeviceIdType.MESH
+        )
+    pl.semaphore_wait(barrier, len(peers))
+
+    sent = []
+
+    def send(*args):
+        copy = remote(*args)
+        copy.start()
+        sent.append(copy)
+
+    for d in range(1, rows):
+        send(kv_own, kv_all.at[me], kv_zsem.at[d], kv_rsem.at[me], place(z_at(d), y, c))
+    send(kv_own, kv_all.at[me], kv_ysem.at[0], kv_rsem.at[me], y_peer)
+    send(kv_own, kv_all.at[me], kv_csem.at[0], kv_rsem.at[me], c_peer)
+
+    def kv_wait(slot):
+        remote(kv_all.at[slot], kv_all.at[slot], kv_zsem.at[0], kv_rsem.at[slot], c_peer).wait_recv()
+
+    token = lax.broadcasted_iota(jnp.int32, (tok_rows, 1), 0)
+    starts = jnp.zeros((tok_rows, 1), jnp.int32)
+    ends = jnp.zeros((tok_rows, 1), jnp.int32)
+    for r in range(tok_rows // SPAN):
+        mine = (token >= r * SPAN) & (token < (r + 1) * SPAN)
+        starts = jnp.where(mine, offsets[r], starts)
+        ends = jnp.where(mine, offsets[r] + lengths[r] - SPAN + token - r * SPAN, ends)
+    inv_root = 1.0 / math.sqrt(head_dim)
+    lane = lax.broadcasted_iota(jnp.int32, (tok_rows, local_len), 1)
+
+    def scale_line(block, which):
+        first = 2 * local_len + which * scale_rows
+        lines = block[2 * local_len : 2 * local_len + 16, :].astype(f32)
+        at = first - 2 * local_len
+        return jnp.concatenate([lines[at + i : at + i + 1, :] for i in range(scale_rows)], axis=1)
+
+    order = []
+    maxima = []
+
+    def score_block(slot, block):
+        keys = block[0:local_len, :]
+        part = lax.dot_general(
+            queries[...], keys, (((1,), (1,)), ((), ())), preferred_element_type=f32
+        )
+        part = part * (scale_line(block, 0) * inv_root)
+        positions = slot * local_len + lane
+        part = jnp.where((positions >= starts) & (positions <= ends), part, NEG_FILL)
+        scores[len(order)] = part
+        order.append(block)
+        maxima.append(jnp.max(part, axis=1, keepdims=True))
+
+    score_block(me, kv_own)
+    for d in range(1, rows):
+        slot = place(z_at(d), y, c)
+        kv_wait(slot)
+        send(kv_all.at[slot], kv_all.at[slot], kv_ysem.at[d], kv_rsem.at[slot], y_peer)
+        send(kv_all.at[slot], kv_all.at[slot], kv_csem.at[d], kv_rsem.at[slot], c_peer)
+        score_block(slot, kv_all.at[slot])
+    for d in range(rows):
+        slot = place(z_at(d), 1 - y, c)
+        kv_wait(slot)
+        send(kv_all.at[slot], kv_all.at[slot], kv_csem.at[rows + d], kv_rsem.at[slot], c_peer)
+        score_block(slot, kv_all.at[slot])
+    for yy in (y, 1 - y):
+        for d in range(rows):
+            slot = place(z_at(d), yy, 1 - c)
+            kv_wait(slot)
+            score_block(slot, kv_all.at[slot])
+
+    row_max = functools.reduce(jnp.maximum, maxima)
+    numerator = jnp.zeros((tok_rows, head_dim), f32)
+    denominator = jnp.zeros((tok_rows, 1), f32)
+    for step, block in enumerate(order):
+        weights = jnp.exp(scores[step] - row_max)
+        denominator = denominator + jnp.sum(weights, axis=1, keepdims=True)
+        probs = (weights * scale_line(block, 1)).astype(bf16)
+        numerator = numerator + jnp.dot(
+            probs, block[local_len : 2 * local_len, :], preferred_element_type=f32
+        )
+    att_all[z] = (numerator / denominator).astype(bf16)
+
+    for d in range(1, rows):
+        send(att_all.at[z], att_all.at[z], att_ssem.at[d], att_rsem.at[z], place(z_at(d), y, c))
+    down = lax.broadcasted_iota(jnp.int32, (head_dim, head_dim), 0)
+    across = lax.broadcasted_iota(jnp.int32, (head_dim, head_dim), 1)
+    common = down & across
+    parity = jnp.zeros((head_dim, head_dim), jnp.int32)
+    for bit in range(head_dim.bit_length() - 1):
+        parity = parity + ((common >> bit) & 1)
+    hd_matrix = jnp.where((parity & 1) == 0, 1.0, -1.0).astype(f32)
+    for d in range(1, rows):
+        zz = z_at(d)
+        remote(att_all.at[zz], att_all.at[zz], att_ssem.at[0], att_rsem.at[zz], y_peer).wait_recv()
+    mixed = jnp.zeros((tok_rows, head_dim), f32)
+    for zz in range(rows):
+        odd = 0
+        for bit in range(rows.bit_length() - 1):
+            if zz >> bit & 1:
+                odd = odd + lax.rem(lax.div(z, 1 << bit), 2)
+        sign = (1 - 2 * lax.rem(odd, 2)).astype(f32) if zz else 1.0
+        mixed = mixed + att_all[zz].astype(f32) * sign
+    for level, (peer, bit) in enumerate(((y_peer, y), (c_peer, c))):
+        mix_send[level] = mixed
+        send(mix_send.at[level], mix_recv.at[level], mix_ssem.at[level], mix_rsem.at[level], peer)
+        sign = (1 - 2 * bit).astype(f32)
+        remote(
+            mix_send.at[level], mix_recv.at[level], mix_ssem.at[level], mix_rsem.at[level], peer
+        ).wait_recv()
+        mixed = mixed * sign + mix_recv[level]
+    rotated = jnp.dot(
+        mixed, hd_matrix, precision=lax.Precision.HIGHEST, preferred_element_type=f32
+    ) * (1.0 / math.sqrt(n * head_dim))
+    limit = clamp_code[0].astype(f32) / 1024.0
+    act = jnp.clip(rotated, -limit, limit).astype(bf16)
+
+    def partial_sum(dest):
+        columns = pl.ds(pl.multiple_of(dest * cols, cols), cols)
+        return jnp.dot(act, w_out[:, columns], preferred_element_type=f32)
+
+    steps = [d for d in range(1, rows)] + [0]
+    for half, yy in enumerate((1 - y, y)):
+        for d in steps:
+            k = half * rows + d
+            core_send[k] = partial_sum(place(z_at(d), yy, 1 - c)).astype(bf16)
+            send(core_send.at[k], core_recv.at[k], core_ssem.at[k], core_rsem.at[k], c_peer)
+        if half == 0:
+            for d in steps:
+                total = partial_sum(place(z_at(d), yy, c))
+                remote(
+                    core_send.at[d], core_recv.at[d], core_ssem.at[d], core_rsem.at[d], c_peer
+                ).wait_recv()
+                y_send[d] = (total + core_recv[d].astype(f32)).astype(bf16)
+                send(y_send.at[d], y_recv.at[d], y_ssem.at[d], y_rsem.at[d], y_peer)
+    total = None
+    for d in steps:
+        k = rows + d
+        total = partial_sum(place(z_at(d), y, c))
+        remote(
+            core_send.at[k], core_recv.at[k], core_ssem.at[k], core_rsem.at[k], c_peer
+        ).wait_recv()
+        total = total + core_recv[k].astype(f32)
+        remote(y_send.at[d], y_recv.at[d], y_ssem.at[d], y_rsem.at[d], y_peer).wait_recv()
+        total = total + y_recv[d].astype(f32)
+        if d:
+            z_send[d] = total.astype(bf16)
+            send(z_send.at[d], z_recv.at[d], z_ssem.at[d], z_rsem.at[d], place(z_at(d), y, c))
+    for d in range(1, rows):
+        remote(z_send.at[d], z_recv.at[d], z_ssem.at[d], z_rsem.at[d], y_peer).wait_recv()
+        total = total + z_recv[d].astype(f32)
+    out[...] = total.T.astype(out.dtype)
+    for copy in sent:
+        copy.wait_send()
+
+
+def fused(n, queries, cache, cache_scale, offsets, lengths, clamp_code, w_out):
+    tok_rows, head_dim = queries.shape
+    local_len = cache.shape[1]
+    rows = n // 4
+    cols = w_out.shape[1] // n
+    scale_rows = 2 * local_len // head_dim
+    kv_own = jnp.concatenate(
+        [
+            cache.reshape(2 * local_len, head_dim),
+            cache_scale.reshape(scale_rows, head_dim),
+            jnp.zeros((16 - scale_rows, head_dim), cache.dtype),
+        ],
+        0,
+    )
+    vmem = pl.BlockSpec(memory_space=pltpu.VMEM)
+    smem = pl.BlockSpec(memory_space=pltpu.SMEM)
+    bf16, f32 = jnp.bfloat16, jnp.float32
+    dma = pltpu.SemaphoreType.DMA
+    block = (tok_rows, cols)
+    return pl.pallas_call(
+        functools.partial(fused_kernel, n),
+        out_shape=jax.ShapeDtypeStruct((cols, tok_rows), bf16),
+        in_specs=[vmem, vmem, smem, smem, smem, vmem],
+        out_specs=vmem,
+        scratch_shapes=[
+            pltpu.VMEM((n,) + kv_own.shape, bf16),
+            pltpu.VMEM((n, tok_rows, local_len), f32),
+            pltpu.VMEM((rows, tok_rows, head_dim), bf16),
+            pltpu.VMEM((2, tok_rows, head_dim), f32),
+            pltpu.VMEM((2, tok_rows, head_dim), f32),
+            pltpu.VMEM((2 * rows,) + block, bf16),
+            pltpu.VMEM((2 * rows,) + block, bf16),
+            pltpu.VMEM((rows,) + block, bf16),
+            pltpu.VMEM((rows,) + block, bf16),
+            pltpu.VMEM((rows,) + block, bf16),
+            pltpu.VMEM((rows,) + block, bf16),
+            dma((rows,)),
+            dma((rows,)),
+            dma((2 * rows,)),
+            dma((n,)),
+            dma((rows,)),
+            dma((rows,)),
+            dma((2,)),
+            dma((2,)),
+            dma((2 * rows,)),
+            dma((2 * rows,)),
+            dma((rows,)),
+            dma((rows,)),
+            dma((rows,)),
+            dma((rows,)),
+        ],
+        compiler_params=pltpu.CompilerParams(
+            collective_id=0, has_side_effects=True, vmem_limit_bytes=40 * 1024 * 1024
+        ),
+        cost_estimate=pl.CostEstimate(
+            flops=2 * tok_rows * head_dim * (2 * n * local_len + w_out.shape[1]),
+            bytes_accessed=2 * w_out.size + 2 * cols * tok_rows,
+            transcendentals=tok_rows * n * local_len,
+        ),
+    )(queries, kv_own, offsets, lengths, clamp_code, w_out)
+
+
+def fits_fused(n, queries, cache, w_out):
+    head_dim, local_len = queries.shape[1], cache.shape[1]
+    return (
+        cache.shape[2] == head_dim
+        and n % 4 == 0
+        and (n & (n - 1)) == 0
+        and local_len % head_dim == 0
+        and 2 * local_len // head_dim <= 16
+        and w_out.shape[1] % (n * 128) == 0
+        and n * local_len <= 16384
+    )
+
+
+def per_device(n, queries, cache, cache_scale, offsets, lengths, clamp_code, w_out):
+    if fits_fused(n, queries, cache, w_out):
+        return fused(n, queries, cache, cache_scale, offsets, lengths, clamp_code, w_out)
     my_index = lax.axis_index("head")
     head_dim = queries.shape[1]
     local_len = cache.shape[1]
@@ -122,7 +421,7 @@
 
 def solution(mesh):
     return jax.shard_map(
-        per_device,
+        functools.partial(per_device, mesh.shape["head"]),
         mesh=mesh,
         in_specs=(
             P("groups", "head"),

time: 253 us -> 79.1 us (0.31)
  waiting for transfers between devices: 124 us -> 0 us
  blocking collectives: 95.3 us -> 0 us
  Pallas kernels: 0 us -> 71.2 us
  between operations: 14.8 us -> 0.68 us
  matrix products: 10.3 us -> 0 us
  other arithmetic: 4.83 us -> 1.04 us
  local copies, waits for them, and re-layouts: 2.38 us -> 5.73 us
    reduce_scatter x2 -> x0, waiting for transfers between devices: 124 us -> none  [the longest x1 102 us: per_device(): lax.psum_scatter(lax.dot_general(w_out, activation, (((0,), (1,)), ((), (...]
    pallas_call x0 -> x1, Pallas kernels: none -> 71.2 us  [fused(): pl.pallas_call(functools.partial(fused_kernel, n), out_shape=jax.ShapeDty...]
    pmax x1 -> x0, blocking collectives: 30.3 us -> none  [per_device(): global_max = lax.pmax(local_max, 'head')]
    unnamed x1 -> x0, blocking collectives: 30.1 us -> none
    all_gather x1 -> x0, blocking collectives: 24.6 us -> none  [per_device(): gathered = lax.all_gather(queries, 'head', axis=1, tiled=True)]
    dot_general x5 -> x0, matrix products: 10.3 us -> none  [the longest x1 6.66 us: per_device(): lax.dot_general(w_out, activation, (((0,), (1,)), ((), ())), preferred_el...]
    all_to_all x1 -> x0, blocking collectives: 10.2 us -> none  [per_device(): lax.all_to_all(clamped, 'head', split_axis=0, concat_axis=1, tiled=True)[0]]
    unnamed x7 -> x9, local copies, waits for them, and re-layouts: 1.53 us -> 4.96 us
  transfers between devices with their start and end apart: 2 -> 0, of which waited for: 2 -> 0; matrix products, arithmetic and copies ran while one was open for 0% -> 0% of each run, Pallas kernels for 0% -> 0%
where the time goes in v1:
time: 79.1 us; the launch traced here: 78.7 us
  Pallas kernels  71.2 us (90%)
  local copies, waits for them, and re-layouts  5.73 us (7%)
  other arithmetic  1.04 us (1%)
    pallas_call x1, Pallas kernels, fused(): pl.pallas_call(functools.partial(fused_kernel, n), out_shape=jax.ShapeDty...  71.2 us
    unnamed x9, local copies, waits for them, and re-layouts  4.96 us

profile of v1, /device:TPU:0, one launch (start us, length us, event | category | flops | bytes accessed | tf_op | source)
XLA Modules:
  0.0 78.7 jit_solution(7600562281757410584)
XLA Ops:
  0.7 0.7 reshape.7
  1.4 0.1 pad.2.clone
  1.4 1.0 %maximum_maximum_fusion.kv_own = bf16[528,128]{1,0:T(8,128)(2,1)S(1)} fusion(bf16[4,128]{1,0:T(4,128)(2,1)S(1)} %reshape.7, bf16[512,128]{1,0:T(8,128)(2,1)} %bitcast.3, bf16[528]{0:T(1024)(128)(2,1)S(1)} %pad.2.clone), kind=kLoop, calls=%fused_computation | loop fusion | flops 405504 | bytes 268320 | tf_op jit(solution)/shard_map/concatenate | solution.py:264
  2.5 0.0 copy-start
  2.5 2.2 %copy-done = bf16[128,16384]{1,0:T(8,128)(2,1)S(1)} copy-done((bf16[128,16384]{1,0:T(8,128)(2,1)S(1)}, bf16[128,16384]{1,0:T(8,128)(2,1)}, u32[]{:S(2)}) %copy-start) | copy-done | bytes 4194328
  4.7 0.0 copy-start.1
  4.7 0.8 copy-done.1
  5.4 0.0 copy-start.2
  5.4 0.7 copy-done.2
  6.1 0.0 copy-start.3
  6.1 0.7 copy-done.3
  6.7 71.2 %shard_map.73 = bf16[1024,128]{1,0:T(8,128)(2,1)S(1)} custom-call(bf16[128,128]{1,0:T(8,128)(2,1)S(1)} %copy-done.1, bf16[528,128]{1,0:T(8,128)(2,1)S(1)} %maximum_maximum_fusion.kv_own, s32[2]{0:T(128)S(1)} %copy-done.2, s32[2]{0:T(128)S(1)} %copy-done.3, s32[1]{0:T(128)S(6)} %copy.9.clamp_code, bf16[128,16384]{1,0:T(8,128)(2,1)S(1)} %copy-done), custom_call_target="tpu_custom_call" | custom-call | flops 805306368 | bytes 4456448 | tf_op jit(solution)/shard_map/pallas_call | solution.py:277
  78.0 0.7 copy.10
  (1 shorter events, 0.0 us)
Async XLA Ops:
  2.5 2.2 %copy-start = (bf16[128,16384]{1,0:T(8,128)(2,1)S(1)}, bf16[128,16384]{1,0:T(8,128)(2,1)}, u32[]{:S(2)}) copy-start(bf16[128,16384]{1,0:T(8,128)(2,1)} %w_out.1) | copy-start | bytes 12582916
  4.7 0.8 copy-start.1
  5.4 0.7 copy-start.2
  6.1 0.7 copy-start.3

commit v2 on v1

--- a/solution.py
+++ b/solution.py
@@ -12,6 +12,8 @@
 
 
 NEG_FILL = -1e30
+
+EARLY = 2
 
 
 def hadamard(matrix_size):
@@ -38,24 +40,35 @@
 
 def fused_kernel(
     n,
+    queries_hbm,
+    cache_hbm,
+    scale_hbm,
+    offsets_hbm,
+    lengths_hbm,
+    clamp_hbm,
+    w_out,
+    out,
     queries,
     kv_own,
+    scale_own,
     offsets,
     lengths,
     clamp_code,
-    w_out,
-    out,
+    w_own,
+    w_quad,
     kv_all,
     scores,
     att_all,
     mix_send,
     mix_recv,
-    core_send,
-    core_recv,
-    y_send,
-    y_recv,
     z_send,
     z_recv,
+    own_sem,
+    w_sem,
+    wq_ssem,
+    wq_rsem,
+    wx_ssem,
+    wx_rsem,
     kv_zsem,
     kv_ysem,
     kv_csem,
@@ -64,20 +77,18 @@
     att_rsem,
     mix_ssem,
     mix_rsem,
-    core_ssem,
-    core_rsem,
-    y_ssem,
-    y_rsem,
     z_ssem,
     z_rsem,
 ):
     f32, bf16 = jnp.float32, jnp.bfloat16
     rows = n // 4
     tok_rows, head_dim = queries.shape
+    half_dim = head_dim // 2
     local_len = (kv_own.shape[0] - 16) // 2
     scale_rows = local_len // head_dim
     cols = out.shape[0]
     me = lax.axis_index("head")
+    group = lax.axis_index("groups")
     z, y, c = lax.div(me, 4), lax.rem(lax.div(me, 2), 2), lax.rem(me, 2)
 
     def place(zz, yy, cc):
@@ -87,15 +98,34 @@
         return lax.rem(z + step, rows)
 
     y_peer, c_peer = place(z, 1 - y, c), place(z, y, 1 - c)
-    peers = [place(z_at(d), y, c) for d in range(1, rows)] + [y_peer, c_peer]
-
-    def remote(src, dst, ssem, rsem, peer):
+    quad = (place(z, y, c), c_peer, y_peer, place(z, 1 - y, 1 - c))
+    peers = [place(z_at(d), y, c) for d in range(1, rows)] + list(quad[1:])
+
+    locals_in = (
+        (cache_hbm.at[0], kv_own.at[pl.ds(0, local_len)]),
+        (cache_hbm.at[1], kv_own.at[pl.ds(local_len, local_len)]),
+        (scale_hbm, scale_own),
+        (queries_hbm, queries),
+        (offsets_hbm, offsets),
+        (lengths_hbm, lengths),
+        (clamp_hbm, clamp_code),
+    )
+    own_copies = [
+        pltpu.make_async_copy(src, dst, own_sem.at[i]) for i, (src, dst) in enumerate(locals_in)
+    ]
+    for copy in own_copies:
+        copy.start()
+
+    def remote(src, dst, ssem, rsem, peer, to_group=None):
+        target = {"head": peer}
+        if to_group is not None:
+            target["groups"] = to_group
         return pltpu.make_async_remote_copy(
             src_ref=src,
             dst_ref=dst,
             send_sem=ssem,
             recv_sem=rsem,
-            device_id={"head": peer},
+            device_id=target,
             device_id_type=pl.DeviceIdType.MESH,
         )
 
@@ -104,7 +134,23 @@
         pl.semaphore_signal(
             barrier, inc=1, device_id={"head": peer}, device_id_type=pl.DeviceIdType.MESH
         )
-    pl.semaphore_wait(barrier, len(peers))
+    pl.semaphore_signal(
+        barrier,
+        inc=1,
+        device_id={"head": me, "groups": 1 - group},
+        device_id_type=pl.DeviceIdType.MESH,
+    )
+    for copy in own_copies[:3]:
+        copy.wait()
+    scale_lines = scale_own[...].astype(f32)
+    lines = [
+        scale_lines[which, :, i * head_dim : (i + 1) * head_dim]
+        for which in range(2)
+        for i in range(scale_rows)
+    ]
+    lines.append(jnp.zeros((16 - len(lines), head_dim), f32))
+    kv_own[2 * local_len : 2 * local_len + 16, :] = jnp.concatenate(lines, axis=0).astype(bf16)
+    pl.semaphore_wait(barrier, len(peers) + 1)
 
     sent = []
 
@@ -118,9 +164,65 @@
     send(kv_own, kv_all.at[me], kv_ysem.at[0], kv_rsem.at[me], y_peer)
     send(kv_own, kv_all.at[me], kv_csem.at[0], kv_rsem.at[me], c_peer)
 
+    def w_columns(d, yy, cc):
+        row = z_at(d - d % 2)
+        row = row + (1 - 2 * lax.rem(row, 2)) * (d % 2)
+        return pl.ds(pl.multiple_of(place(row, yy, cc) * cols, cols), cols)
+
+    quad_at = ((y, c), (y, 1 - c), (1 - y, c), (1 - y, 1 - c))
+    my_half = pl.ds(pl.multiple_of(group * half_dim, half_dim), half_dim)
+
+    other_half = pl.ds(pl.multiple_of((1 - group) * half_dim, half_dim), half_dim)
+
+    def w_share(d):
+        for k in (2, 3):
+            send(
+                w_out.at[my_half, w_columns(d, *quad_at[k])],
+                w_quad.at[k - 1, d, my_half],
+                wq_ssem.at[k - 1, d],
+                wq_rsem.at[k - 1, d],
+                quad[k],
+            )
+
+    def w_core(d):
+        send(
+            w_out.at[:, w_columns(d, *quad_at[1])],
+            w_quad.at[0, d],
+            wq_ssem.at[0, d],
+            wq_rsem.at[0, d],
+            quad[1],
+        )
+
+    def w_forward(d):
+        for k in (1, 2):
+            mine = w_quad.at[k, d, my_half]
+            remote(mine, mine, wq_ssem.at[k, d], wq_rsem.at[k, d], y_peer).wait_recv()
+            send(mine, mine, wx_ssem.at[k, d], wx_rsem.at[k, d], me, 1 - group)
+
+    def w_wait(d):
+        full = w_quad.at[0, d]
+        remote(full, full, wq_ssem.at[0, d], wq_rsem.at[0, d], y_peer).wait_recv()
+        for k in (1, 2):
+            half = w_quad.at[k, d, other_half]
+            remote(half, half, wx_ssem.at[k, d], wx_rsem.at[k, d], me, 1 - group).wait_recv()
+
+    steps = [d for p in range(1, rows // 2) for d in (2 * p + 1, 2 * p)] + [1, 0]
+    w_copies = [
+        pltpu.make_async_copy(w_out.at[:, w_columns(d, y, c)], w_own.at[d], w_sem.at[d])
+        for d in range(rows)
+    ]
+    for copy in w_copies:
+        copy.start()
+    for d in steps[:EARLY]:
+        w_share(d)
+    for d in steps:
+        w_core(d)
+
     def kv_wait(slot):
         remote(kv_all.at[slot], kv_all.at[slot], kv_zsem.at[0], kv_rsem.at[slot], c_peer).wait_recv()
 
+    for copy in own_copies[3:]:
+        copy.wait()
     token = lax.broadcasted_iota(jnp.int32, (tok_rows, 1), 0)
     starts = jnp.zeros((tok_rows, 1), jnp.int32)
     ends = jnp.zeros((tok_rows, 1), jnp.int32)
@@ -164,6 +266,10 @@
         kv_wait(slot)
         send(kv_all.at[slot], kv_all.at[slot], kv_csem.at[rows + d], kv_rsem.at[slot], c_peer)
         score_block(slot, kv_all.at[slot])
+    for d in steps[EARLY:]:
+        w_share(d)
+    for d in steps[:EARLY]:
+        w_forward(d)
     for yy in (y, 1 - y):
         for d in range(rows):
             slot = place(z_at(d), yy, 1 - c)
@@ -184,6 +290,8 @@
 
     for d in range(1, rows):
         send(att_all.at[z], att_all.at[z], att_ssem.at[d], att_rsem.at[z], place(z_at(d), y, c))
+    for d in steps[EARLY:3]:
+        w_forward(d)
     down = lax.broadcasted_iota(jnp.int32, (head_dim, head_dim), 0)
     across = lax.broadcasted_iota(jnp.int32, (head_dim, head_dim), 1)
     common = down & across
@@ -202,54 +310,71 @@
                 odd = odd + lax.rem(lax.div(z, 1 << bit), 2)
         sign = (1 - 2 * lax.rem(odd, 2)).astype(f32) if zz else 1.0
         mixed = mixed + att_all[zz].astype(f32) * sign
-    for level, (peer, bit) in enumerate(((y_peer, y), (c_peer, c))):
-        mix_send[level] = mixed
-        send(mix_send.at[level], mix_recv.at[level], mix_ssem.at[level], mix_rsem.at[level], peer)
-        sign = (1 - 2 * bit).astype(f32)
+    mixed = jnp.dot(mixed, hd_matrix, precision=lax.Precision.HIGHEST, preferred_element_type=f32)
+
+    def swap(at, size, level, peer):
+        there = remote(
+            mix_send.at[pl.ds(at, size)],
+            mix_recv.at[pl.ds(at, size)],
+            mix_ssem.at[level],
+            mix_rsem.at[level],
+            peer,
+        )
+        there.start()
+        sent.append(there)
+        return there
+
+    mix_send[0] = mixed
+    there = swap(0, 1, 0, y_peer)
+    for d in steps[max(EARLY, 3):]:
+        w_forward(d)
+    there.wait_recv()
+    y_sign, c_sign = (1 - 2 * y).astype(f32), (1 - 2 * c).astype(f32)
+    pair = (mixed * y_sign + mix_recv[0], mixed - mix_recv[0] * y_sign)
+    mix_send[1] = pair[0]
+    mix_send[2] = pair[1]
+    there = swap(1, 2, 1, c_peer)
+    there.wait_recv()
+    limit = clamp_code[0].astype(f32) / 1024.0
+    scale_out = 1.0 / math.sqrt(n * head_dim)
+    acts = []
+    for i in range(2):
+        for full in (pair[i] * c_sign + mix_recv[1 + i], pair[i] - mix_recv[1 + i] * c_sign):
+            acts.append(jnp.clip(full * scale_out, -limit, limit).astype(bf16))
+
+    def row_sum(d):
+        w_copies[d].wait()
+        w_wait(d)
+        total = jnp.dot(acts[0], w_own[d], preferred_element_type=f32)
+        for k in range(3):
+            total = total + jnp.dot(acts[k + 1], w_quad[k, d], preferred_element_type=f32)
+        return total
+
+    def z_wait(slot, peer):
         remote(
-            mix_send.at[level], mix_recv.at[level], mix_ssem.at[level], mix_rsem.at[level], peer
+            z_send.at[slot], z_recv.at[slot], z_ssem.at[slot], z_rsem.at[slot], peer
         ).wait_recv()
-        mixed = mixed * sign + mix_recv[level]
-    rotated = jnp.dot(
-        mixed, hd_matrix, precision=lax.Precision.HIGHEST, preferred_element_type=f32
-    ) * (1.0 / math.sqrt(n * head_dim))
-    limit = clamp_code[0].astype(f32) / 1024.0
-    act = jnp.clip(rotated, -limit, limit).astype(bf16)
-
-    def partial_sum(dest):
-        columns = pl.ds(pl.multiple_of(dest * cols, cols), cols)
-        return jnp.dot(act, w_out[:, columns], preferred_element_type=f32)
-
-    steps = [d for d in range(1, rows)] + [0]
-    for half, yy in enumerate((1 - y, y)):
-        for d in steps:
-            k = half * rows + d
-            core_send[k] = partial_sum(place(z_at(d), yy, 1 - c)).astype(bf16)
-            send(core_send.at[k], core_recv.at[k], core_ssem.at[k], core_rsem.at[k], c_peer)
-        if half == 0:
-            for d in steps:
-                total = partial_sum(place(z_at(d), yy, c))
-                remote(
-                    core_send.at[d], core_recv.at[d], core_ssem.at[d], core_rsem.at[d], c_peer
-                ).wait_recv()
-                y_send[d] = (total + core_recv[d].astype(f32)).astype(bf16)
-                send(y_send.at[d], y_recv.at[d], y_ssem.at[d], y_rsem.at[d], y_peer)
-    total = None
-    for d in steps:
-        k = rows + d
-        total = partial_sum(place(z_at(d), y, c))
-        remote(
-            core_send.at[k], core_recv.at[k], core_ssem.at[k], core_rsem.at[k], c_peer
-        ).wait_recv()
-        total = total + core_recv[k].astype(f32)
-        remote(y_send.at[d], y_recv.at[d], y_ssem.at[d], y_rsem.at[d], y_peer).wait_recv()
-        total = total + y_recv[d].astype(f32)
-        if d:
-            z_send[d] = total.astype(bf16)
-            send(z_send.at[d], z_recv.at[d], z_ssem.at[d], z_rsem.at[d], place(z_at(d), y, c))
-    for d in range(1, rows):
-        remote(z_send.at[d], z_recv.at[d], z_ssem.at[d], z_rsem.at[d], y_peer).wait_recv()
-        total = total + z_recv[d].astype(f32)
+        return z_recv[slot].astype(f32)
+
+    def z_go(slot, value, peer):
+        z_send[slot] = value.astype(bf16)
+        send(z_send.at[slot], z_recv.at[slot], z_ssem.at[slot], z_rsem.at[slot], peer)
+
+    far = rows // 2 - 1
+    low = lax.rem(z, 2)
+    z_mate = place(z + 1 - 2 * low, y, c)
+    for p in range(1, far + 1):
+        z_go(p - 1, row_sum(2 * p + 1), z_mate)
+    kept = [row_sum(2 * p) for p in range(1, far + 1)]
+    near = row_sum(1)
+    for p in range(1, far + 1):
+        peer = place(z_at(2 * p), y, c)
+        z_go(far + p - 1, kept[p - 1] + z_wait(p - 1, z_mate), peer)
+    z_go(2 * far, near, z_mate)
+    total = row_sum(0)
+    total = total + z_wait(2 * far, z_mate)
+    for p in range(1, far + 1):
+        total = total + z_wait(far + p - 1, z_mate)
     out[...] = total.T.astype(out.dtype)
     for copy in sent:
         copy.wait_send()
@@ -260,37 +385,39 @@
     local_len = cache.shape[1]
     rows = n // 4
     cols = w_out.shape[1] // n
-    scale_rows = 2 * local_len // head_dim
-    kv_own = jnp.concatenate(
-        [
-            cache.reshape(2 * local_len, head_dim),
-            cache_scale.reshape(scale_rows, head_dim),
-            jnp.zeros((16 - scale_rows, head_dim), cache.dtype),
-        ],
-        0,
-    )
+    kv_shape = (2 * local_len + 16, head_dim)
     vmem = pl.BlockSpec(memory_space=pltpu.VMEM)
-    smem = pl.BlockSpec(memory_space=pltpu.SMEM)
+    hbm = pl.BlockSpec(memory_space=pltpu.HBM)
     bf16, f32 = jnp.bfloat16, jnp.float32
     dma = pltpu.SemaphoreType.DMA
     block = (tok_rows, cols)
     return pl.pallas_call(
         functools.partial(fused_kernel, n),
         out_shape=jax.ShapeDtypeStruct((cols, tok_rows), bf16),
-        in_specs=[vmem, vmem, smem, smem, smem, vmem],
+        in_specs=[hbm] * 7,
         out_specs=vmem,
         scratch_shapes=[
-            pltpu.VMEM((n,) + kv_own.shape, bf16),
+            pltpu.VMEM(queries.shape, bf16),
+            pltpu.VMEM(kv_shape, bf16),
+            pltpu.VMEM(cache_scale.shape, bf16),
+            pltpu.SMEM(offsets.shape, jnp.int32),
+            pltpu.SMEM(lengths.shape, jnp.int32),
+            pltpu.SMEM(clamp_code.shape, jnp.int32),
+            pltpu.VMEM((rows, head_dim, cols), bf16),
+            pltpu.VMEM((3, rows, head_dim, cols), bf16),
+            pltpu.VMEM((n,) + kv_shape, bf16),
             pltpu.VMEM((n, tok_rows, local_len), f32),
             pltpu.VMEM((rows, tok_rows, head_dim), bf16),
-            pltpu.VMEM((2, tok_rows, head_dim), f32),
-            pltpu.VMEM((2, tok_rows, head_dim), f32),
-            pltpu.VMEM((2 * rows,) + block, bf16),
-            pltpu.VMEM((2 * rows,) + block, bf16),
+            pltpu.VMEM((3, tok_rows, head_dim), f32),
+            pltpu.VMEM((3, tok_rows, head_dim), f32),
             pltpu.VMEM((rows,) + block, bf16),
             pltpu.VMEM((rows,) + block, bf16),
-            pltpu.VMEM((rows,) + block, bf16),
-            pltpu.VMEM((rows,) + block, bf16),
+            dma((7,)),
+            dma((rows,)),
+            dma((3, rows)),
+            dma((3, rows)),
+            dma((3, rows)),
+            dma((3, rows)),
             dma((rows,)),
             dma((rows,)),
             dma((2 * rows,)),
@@ -299,10 +426,6 @@
             dma((rows,)),
             dma((2,)),
             dma((2,)),
-            dma((2 * rows,)),
-            dma((2 * rows,)),
-            dma((rows,)),
-            dma((rows,)),
             dma((rows,)),
             dma((rows,)),
         ],
@@ -314,14 +437,17 @@
             bytes_accessed=2 * w_out.size + 2 * cols * tok_rows,
             transcendentals=tok_rows * n * local_len,
         ),
-    )(queries, kv_own, offsets, lengths, clamp_code, w_out)
-
-
-def fits_fused(n, queries, cache, w_out):
+    )(queries, cache, cache_scale, offsets, lengths, clamp_code, w_out)
+
+
+def fits_fused(groups, n, queries, cache, w_out):
     head_dim, local_len = queries.shape[1], cache.shape[1]
     return (
-        cache.shape[2] == head_dim
+        groups == 2
+        and cache.shape[2] == head_dim
+        and head_dim % 32 == 0
         and n % 4 == 0
+        and n >= 16
         and (n & (n - 1)) == 0
         and local_len % head_dim == 0
         and 2 * local_len // head_dim <= 16
@@ -330,8 +456,8 @@
     )
 
 
-def per_device(n, queries, cache, cache_scale, offsets, lengths, clamp_code, w_out):
-    if fits_fused(n, queries, cache, w_out):
+def per_device(groups, n, queries, cache, cache_scale, offsets, lengths, clamp_code, w_out):
+    if fits_fused(groups, n, queries, cache, w_out):
         return fused(n, queries, cache, cache_scale, offsets, lengths, clamp_code, w_out)
     my_index = lax.axis_index("head")
     head_dim = queries.shape[1]
@@ -421,7 +547,7 @@
 
 def solution(mesh):
     return jax.shard_map(
-        functools.partial(per_device, mesh.shape["head"]),
+        functools.partial(per_device, mesh.shape["groups"], mesh.shape["head"]),
         mesh=mesh,
         in_specs=(
             P("groups", "head"),

time: 79.1 us -> 75.3 us (0.952)
  Pallas kernels: 71.2 us -> 67.8 us
  other arithmetic: 1.04 us -> 0 us
  local copies, waits for them, and re-layouts: 5.73 us -> 6.55 us
    pallas_call x1, Pallas kernels: 71.2 us -> 67.8 us  [fused(): pl.pallas_call(functools.partial(fused_kernel, n), out_shape=jax.ShapeDty...]
    unnamed x9 -> x12, local copies, waits for them, and re-layouts: 4.96 us -> 6.55 us
    concatenate x1 -> x0, other arithmetic: 1.04 us -> none  [fused(): jnp.concatenate([cache.reshape(2 * local_len, head_dim), cache_scale.resh...]
where the time goes in v2:
time: 75.3 us; the launch traced here: 75 us
  Pallas kernels  67.8 us (90%)
  local copies, waits for them, and re-layouts  6.55 us (9%)
    pallas_call x1, Pallas kernels, fused(): pl.pallas_call(functools.partial(fused_kernel, n), out_shape=jax.ShapeDty...  67.8 us
    unnamed x12, local copies, waits for them, and re-layouts  6.55 us

profile of v2, /device:TPU:0, one launch (start us, length us, event | category | flops | bytes accessed | tf_op | source)
XLA Modules:
  0.0 75.0 jit_solution(5508683736840317365)
XLA Ops:
  0.7 0.7 copy.8.scale_hbm
  1.3 0.0 copy-start
  1.3 2.2 %copy-done = bf16[128,16384]{1,0:T(8,128)(2,1)S(1)} copy-done((bf16[128,16384]{1,0:T(8,128)(2,1)S(1)}, bf16[128,16384]{1,0:T(8,128)(2,1)}, u32[]{:S(2)}) %copy-start) | copy-done | bytes 4194328
  3.5 0.0 copy-start.1
  3.5 0.9 %copy-done.1 = bf16[2,256,128]{2,1,0:T(8,128)(2,1)S(1)} copy-done((bf16[2,256,128]{2,1,0:T(8,128)(2,1)S(1)}, bf16[2,256,128]{2,1,0:T(8,128)(2,1)}, u32[]{:S(2)}) %copy-start.1) | copy-done | bytes 131096
  4.4 0.0 copy-start.2
  4.4 0.8 %copy-done.2 = bf16[128,128]{1,0:T(8,128)(2,1)S(1)} copy-done((bf16[128,128]{1,0:T(8,128)(2,1)S(1)}, bf16[128,128]{1,0:T(8,128)(2,1)}, u32[]{:S(2)}) %copy-start.2) | copy-done | bytes 32792
  5.2 0.0 copy-start.3
  5.2 0.7 copy-done.3
  5.8 0.0 copy-start.4
  5.8 0.7 copy-done.4
  6.5 67.8 %shard_map.73 = bf16[1024,128]{1,0:T(8,128)(2,1)S(1)} custom-call(bf16[128,128]{1,0:T(8,128)(2,1)S(1)} %copy-done.2, bf16[2,256,128]{2,1,0:T(8,128)(2,1)S(1)} %copy-done.1, bf16[2,1,256]{2,1,0:T(2,128)(2,1)S(1)} %copy.8.scale_hbm, s32[2]{0:T(128)S(1)} %copy-done.3, s32[2]{0:T(128)S(1)} %copy-done.4, s32[1]{0:T(128)S(6)} %copy.10.clamp_hbm, ...), custom_call_target="tpu_custom_call" | custom-call | flops 805306368 | bytes 4456448 | tf_op jit(solution)/shard_map/pallas_call | solution.py:394
  74.3 0.7 copy.11
Async XLA Ops:
  1.3 2.2 %copy-start = (bf16[128,16384]{1,0:T(8,128)(2,1)S(1)}, bf16[128,16384]{1,0:T(8,128)(2,1)}, u32[]{:S(2)}) copy-start(bf16[128,16384]{1,0:T(8,128)(2,1)} %w_out.1) | copy-start | bytes 12582916
  3.5 0.9 %copy-start.1 = (bf16[2,256,128]{2,1,0:T(8,128)(2,1)S(1)}, bf16[2,256,128]{2,1,0:T(8,128)(2,1)}, u32[]{:S(2)}) copy-start(bf16[2,256,128]{2,1,0:T(8,128)(2,1)} %cache_hbm.1) | copy-start | bytes 393220
  4.4 0.8 %copy-start.2 = (bf16[128,128]{1,0:T(8,128)(2,1)S(1)}, bf16[128,128]{1,0:T(8,128)(2,1)}, u32[]{:S(2)}) copy-start(bf16[128,128]{1,0:T(8,128)(2,1)} %queries_hbm.1) | copy-start | bytes 98308
  5.2 0.7 copy-start.3
  5.8 0.7 copy-start.4

commit v3 on v2

--- a/solution.py
+++ b/solution.py
@@ -13,7 +13,9 @@
 
 NEG_FILL = -1e30
 
-EARLY = 2
+EARLY = 1
+
+LATE = 2
 
 
 def hadamard(matrix_size):
@@ -63,6 +65,8 @@
     mix_recv,
     z_send,
     z_recv,
+    y_send,
+    y_recv,
     own_sem,
     w_sem,
     wq_ssem,
@@ -79,6 +83,8 @@
     mix_rsem,
     z_ssem,
     z_rsem,
+    y_ssem,
+    y_rsem,
 ):
     f32, bf16 = jnp.float32, jnp.bfloat16
     rows = n // 4
@@ -202,21 +208,37 @@
     def w_wait(d):
         full = w_quad.at[0, d]
         remote(full, full, wq_ssem.at[0, d], wq_rsem.at[0, d], y_peer).wait_recv()
-        for k in (1, 2):
+        for k in (1, 2) if d in shared else ():
             half = w_quad.at[k, d, other_half]
             remote(half, half, wx_ssem.at[k, d], wx_rsem.at[k, d], me, 1 - group).wait_recv()
 
     steps = [d for p in range(1, rows // 2) for d in (2 * p + 1, 2 * p)] + [1, 0]
+    late = steps[len(steps) - LATE :]
+    shared = steps[: len(steps) - LATE]
     w_copies = [
         pltpu.make_async_copy(w_out.at[:, w_columns(d, y, c)], w_own.at[d], w_sem.at[d])
         for d in range(rows)
     ]
-    for copy in w_copies:
+    late_copies = {
+        d: pltpu.make_async_copy(
+            w_out.at[:, w_columns(d, 1 - y, c)], w_quad.at[1, d], w_sem.at[rows + d]
+        )
+        for d in late
+    }
+    for copy in w_copies + list(late_copies.values()):
         copy.start()
-    for d in steps[:EARLY]:
+    for d in shared[:EARLY]:
         w_share(d)
     for d in steps:
         w_core(d)
+    for d in late:
+        send(
+            w_out.at[:, w_columns(d, 1 - y, 1 - c)],
+            w_quad.at[2, d],
+            wq_ssem.at[2, d],
+            wq_rsem.at[2, d],
+            c_peer,
+        )
 
     def kv_wait(slot):
         remote(kv_all.at[slot], kv_all.at[slot], kv_zsem.at[0], kv_rsem.at[slot], c_peer).wait_recv()
@@ -266,9 +288,9 @@
         kv_wait(slot)
         send(kv_all.at[slot], kv_all.at[slot], kv_csem.at[rows + d], kv_rsem.at[slot], c_peer)
         score_block(slot, kv_all.at[slot])
-    for d in steps[EARLY:]:
+    for d in shared[EARLY:]:
         w_share(d)
-    for d in steps[:EARLY]:
+    for d in shared[:EARLY]:
         w_forward(d)
     for yy in (y, 1 - y):
         for d in range(rows):
@@ -290,7 +312,7 @@
 
     for d in range(1, rows):
         send(att_all.at[z], att_all.at[z], att_ssem.at[d], att_rsem.at[z], place(z_at(d), y, c))
-    for d in steps[EARLY:3]:
+    for d in shared[EARLY:3]:
         w_forward(d)
     down = lax.broadcasted_iota(jnp.int32, (head_dim, head_dim), 0)
     across = lax.broadcasted_iota(jnp.int32, (head_dim, head_dim), 1)
@@ -326,7 +348,7 @@
 
     mix_send[0] = mixed
     there = swap(0, 1, 0, y_peer)
-    for d in steps[max(EARLY, 3):]:
+    for d in shared[max(EARLY, 3):]:
         w_forward(d)
     there.wait_recv()
     y_sign, c_sign = (1 - 2 * y).astype(f32), (1 - 2 * c).astype(f32)
@@ -346,6 +368,10 @@
         w_copies[d].wait()
         w_wait(d)
         total = jnp.dot(acts[0], w_own[d], preferred_element_type=f32)
+        if d in late:
+            total = total + jnp.dot(acts[1], w_quad[0, d], preferred_element_type=f32)
+            remote(y_send.at[d], y_recv.at[d], y_ssem.at[d], y_rsem.at[d], y_peer).wait_recv()
+            return total + y_recv[d].astype(f32)
         for k in range(3):
             total = total + jnp.dot(acts[k + 1], w_quad[k, d], preferred_element_type=f32)
         return total
@@ -365,6 +391,14 @@
     z_mate = place(z + 1 - 2 * low, y, c)
     for p in range(1, far + 1):
         z_go(p - 1, row_sum(2 * p + 1), z_mate)
+    for d in late:
+        late_copies[d].wait()
+        full = w_quad.at[2, d]
+        remote(full, full, wq_ssem.at[2, d], wq_rsem.at[2, d], c_peer).wait_recv()
+        theirs = jnp.dot(acts[0], w_quad[1, d], preferred_element_type=f32)
+        theirs = theirs + jnp.dot(acts[1], w_quad[2, d], preferred_element_type=f32)
+        y_send[d] = theirs.astype(bf16)
+        send(y_send.at[d], y_recv.at[d], y_ssem.at[d], y_rsem.at[d], y_peer)
     kept = [row_sum(2 * p) for p in range(1, far + 1)]
     near = row_sum(1)
     for p in range(1, far + 1):
@@ -412,8 +446,10 @@
             pltpu.VMEM((3, tok_rows, head_dim), f32),
             pltpu.VMEM((rows,) + block, bf16),
             pltpu.VMEM((rows,) + block, bf16),
+            pltpu.VMEM((rows,) + block, bf16),
+            pltpu.VMEM((rows,) + block, bf16),
             dma((7,)),
-            dma((rows,)),
+            dma((2 * rows,)),
             dma((3, rows)),
             dma((3, rows)),
             dma((3, rows)),
@@ -426,6 +462,8 @@
             dma((rows,)),
             dma((2,)),
             dma((2,)),
+            dma((rows,)),
+            dma((rows,)),
             dma((rows,)),
             dma((rows,)),
         ],

time: 75.3 us -> 69.6 us (0.924)
  Pallas kernels: 67.8 us -> 62.1 us
    pallas_call x1, Pallas kernels: 67.8 us -> 62.1 us  [fused(): pl.pallas_call(functools.partial(fused_kernel, n), out_shape=jax.ShapeDty...]
where the time goes in v3:
time: 69.6 us; the launch traced here: 69.3 us
  Pallas kernels  62.1 us (89%)
  local copies, waits for them, and re-layouts  6.55 us (9%)
    pallas_call x1, Pallas kernels, fused(): pl.pallas_call(functools.partial(fused_kernel, n), out_shape=jax.ShapeDty...  62.1 us
    unnamed x12, local copies, waits for them, and re-layouts  6.55 us

profile of v3, /device:TPU:0, one launch (start us, length us, event | category | flops | bytes accessed | tf_op | source)
XLA Modules:
  0.0 69.3 jit_solution(10324992013943495979)
XLA Ops:
  0.7 0.7 copy.8.scale_hbm
  1.3 0.0 copy-start
  1.3 2.2 %copy-done = bf16[128,16384]{1,0:T(8,128)(2,1)S(1)} copy-done((bf16[128,16384]{1,0:T(8,128)(2,1)S(1)}, bf16[128,16384]{1,0:T(8,128)(2,1)}, u32[]{:S(2)}) %copy-start) | copy-done | bytes 4194328
  3.5 0.0 copy-start.1
  3.5 0.9 %copy-done.1 = bf16[2,256,128]{2,1,0:T(8,128)(2,1)S(1)} copy-done((bf16[2,256,128]{2,1,0:T(8,128)(2,1)S(1)}, bf16[2,256,128]{2,1,0:T(8,128)(2,1)}, u32[]{:S(2)}) %copy-start.1) | copy-done | bytes 131096
  4.4 0.0 copy-start.2
  4.4 0.8 %copy-done.2 = bf16[128,128]{1,0:T(8,128)(2,1)S(1)} copy-done((bf16[128,128]{1,0:T(8,128)(2,1)S(1)}, bf16[128,128]{1,0:T(8,128)(2,1)}, u32[]{:S(2)}) %copy-start.2) | copy-done | bytes 32792
  5.2 0.0 copy-start.3
  5.2 0.7 copy-done.3
  5.8 0.0 copy-start.4
  5.8 0.7 copy-done.4
  6.5 62.1 %shard_map.73 = bf16[1024,128]{1,0:T(8,128)(2,1)S(1)} custom-call(bf16[128,128]{1,0:T(8,128)(2,1)S(1)} %copy-done.2, bf16[2,256,128]{2,1,0:T(8,128)(2,1)S(1)} %copy-done.1, bf16[2,1,256]{2,1,0:T(2,128)(2,1)S(1)} %copy.8.scale_hbm, s32[2]{0:T(128)S(1)} %copy-done.3, s32[2]{0:T(128)S(1)} %copy-done.4, s32[1]{0:T(128)S(6)} %copy.10.clamp_hbm, ...), custom_call_target="tpu_custom_call" | custom-call | flops 805306368 | bytes 4456448 | tf_op jit(solution)/shard_map/pallas_call | solution.py:428
  68.6 0.7 %copy.11 = bf16[1024,128]{1,0:T(8,128)(2,1)} copy(bf16[1024,128]{1,0:T(8,128)(2,1)S(1)} %shard_map.73) | data formatting | bytes 524288
Async XLA Ops:
  1.3 2.2 %copy-start = (bf16[128,16384]{1,0:T(8,128)(2,1)S(1)}, bf16[128,16384]{1,0:T(8,128)(2,1)}, u32[]{:S(2)}) copy-start(bf16[128,16384]{1,0:T(8,128)(2,1)} %w_out.1) | copy-start | bytes 12582916
  3.5 0.9 %copy-start.1 = (bf16[2,256,128]{2,1,0:T(8,128)(2,1)S(1)}, bf16[2,256,128]{2,1,0:T(8,128)(2,1)}, u32[]{:S(2)}) copy-start(bf16[2,256,128]{2,1,0:T(8,128)(2,1)} %cache_hbm.1) | copy-start | bytes 393220
  4.4 0.8 %copy-start.2 = (bf16[128,128]{1,0:T(8,128)(2,1)S(1)}, bf16[128,128]{1,0:T(8,128)(2,1)}, u32[]{:S(2)}) copy-start(bf16[128,128]{1,0:T(8,128)(2,1)} %queries_hbm.1) | copy-start | bytes 98308
  5.2 0.7 copy-start.3
  5.8 0.7 copy-start.4

commit v4 on v3

--- a/solution.py
+++ b/solution.py
@@ -165,8 +165,10 @@
         copy.start()
         sent.append(copy)
 
-    for d in range(1, rows):
+    kv_steps = [d for d in range(1, rows) if 2 * d != rows]
+    for d in kv_steps:
         send(kv_own, kv_all.at[me], kv_zsem.at[d], kv_rsem.at[me], place(z_at(d), y, c))
+    first_sends = list(sent)
     send(kv_own, kv_all.at[me], kv_ysem.at[0], kv_rsem.at[me], y_peer)
     send(kv_own, kv_all.at[me], kv_csem.at[0], kv_rsem.at[me], c_peer)
 
@@ -277,7 +279,13 @@
         maxima.append(jnp.max(part, axis=1, keepdims=True))
 
     score_block(me, kv_own)
-    for d in range(1, rows):
+    for copy in first_sends:
+        copy.wait_send()
+        sent.remove(copy)
+    d = rows // 2
+    kv_steps.append(d)
+    send(kv_own, kv_all.at[me], kv_zsem.at[d], kv_rsem.at[me], place(z_at(d), y, c))
+    for d in kv_steps:
         slot = place(z_at(d), y, c)
         kv_wait(slot)
         send(kv_all.at[slot], kv_all.at[slot], kv_ysem.at[d], kv_rsem.at[slot], y_peer)

time: 69.6 us -> 66.7 us (0.958)
  Pallas kernels: 62.1 us -> 59.2 us
    pallas_call x1, Pallas kernels: 62.1 us -> 59.2 us  [fused(): pl.pallas_call(functools.partial(fused_kernel, n), out_shape=jax.ShapeDty...]
where the time goes in v4:
time: 66.7 us; the launch traced here: 66.4 us
  Pallas kernels  59.2 us (89%)
  local copies, waits for them, and re-layouts  6.55 us (10%)
  between operations  0.67 us (1%)
    pallas_call x1, Pallas kernels, fused(): pl.pallas_call(functools.partial(fused_kernel, n), out_shape=jax.ShapeDty...  59.2 us
    unnamed x12, local copies, waits for them, and re-layouts  6.55 us

profile of v4, /device:TPU:0, one launch (start us, length us, event | category | flops | bytes accessed | tf_op | source)
XLA Modules:
  0.0 66.4 jit_solution(1043714579106252634)
XLA Ops:
  0.7 0.7 %copy.8.scale_hbm = bf16[2,1,256]{2,1,0:T(2,128)(2,1)S(1)} copy(bf16[2,1,256]{2,0,1:T(2,128)(2,1)} %param.9) | data formatting | bytes 2048 | tf_op args[2]
  1.3 0.0 copy-start
  1.3 2.2 %copy-done = bf16[128,16384]{1,0:T(8,128)(2,1)S(1)} copy-done((bf16[128,16384]{1,0:T(8,128)(2,1)S(1)}, bf16[128,16384]{1,0:T(8,128)(2,1)}, u32[]{:S(2)}) %copy-start) | copy-done | bytes 4194328
  3.5 0.0 copy-start.1
  3.5 0.9 %copy-done.1 = bf16[2,256,128]{2,1,0:T(8,128)(2,1)S(1)} copy-done((bf16[2,256,128]{2,1,0:T(8,128)(2,1)S(1)}, bf16[2,256,128]{2,1,0:T(8,128)(2,1)}, u32[]{:S(2)}) %copy-start.1) | copy-done | bytes 131096
  4.4 0.0 copy-start.2
  4.4 0.8 %copy-done.2 = bf16[128,128]{1,0:T(8,128)(2,1)S(1)} copy-done((bf16[128,128]{1,0:T(8,128)(2,1)S(1)}, bf16[128,128]{1,0:T(8,128)(2,1)}, u32[]{:S(2)}) %copy-start.2) | copy-done | bytes 32792
  5.2 0.0 copy-start.3
  5.2 0.7 copy-done.3
  5.8 0.0 copy-start.4
  5.8 0.7 copy-done.4
  6.5 59.2 %shard_map.73 = bf16[1024,128]{1,0:T(8,128)(2,1)S(1)} custom-call(bf16[128,128]{1,0:T(8,128)(2,1)S(1)} %copy-done.2, bf16[2,256,128]{2,1,0:T(8,128)(2,1)S(1)} %copy-done.1, bf16[2,1,256]{2,1,0:T(2,128)(2,1)S(1)} %copy.8.scale_hbm, s32[2]{0:T(128)S(1)} %copy-done.3, s32[2]{0:T(128)S(1)} %copy-done.4, s32[1]{0:T(128)S(6)} %copy.10.clamp_hbm, ...), custom_call_target="tpu_custom_call" | custom-call | flops 805306368 | bytes 4456448 | tf_op jit(solution)/shard_map/pallas_call | solution.py:436
  65.7 0.7 %copy.11 = bf16[1024,128]{1,0:T(8,128)(2,1)} copy(bf16[1024,128]{1,0:T(8,128)(2,1)S(1)} %shard_map.73) | data formatting | bytes 524288
Async XLA Ops:
  1.3 2.2 %copy-start = (bf16[128,16384]{1,0:T(8,128)(2,1)S(1)}, bf16[128,16384]{1,0:T(8,128)(2,1)}, u32[]{:S(2)}) copy-start(bf16[128,16384]{1,0:T(8,128)(2,1)} %w_out.1) | copy-start | bytes 12582916
  3.5 0.9 %copy-start.1 = (bf16[2,256,128]{2,1,0:T(8,128)(2,1)S(1)}, bf16[2,256,128]{2,1,0:T(8,128)(2,1)}, u32[]{:S(2)}) copy-start(bf16[2,256,128]{2,1,0:T(8,128)(2,1)} %cache_hbm.1) | copy-start | bytes 393220
  4.4 0.8 %copy-start.2 = (bf16[128,128]{1,0:T(8,128)(2,1)S(1)}, bf16[128,128]{1,0:T(8,128)(2,1)}, u32[]{:S(2)}) copy-start(bf16[128,128]{1,0:T(8,128)(2,1)} %queries_hbm.1) | copy-start | bytes 98308
  5.2 0.7 copy-start.3
  5.8 0.7 copy-start.4
